TPU v7x, 32 devices: a whole 2x2x4 slice. The times are simulated.
32 devices in a mesh: groups: 2 (over x), tile: 16 (over z, y, core).
Axes of the slice: x: 2, y: 2, z: 4, core: 2. Of those that a mesh axis runs over, the one named last changes fastest.
Arguments:
- walkers: bfloat16 [32, 512, 256], P(('groups', 'tile')), parts along dimension 0, may hold values from -6 to 6
- green_factor: bfloat16 [32, 512, 256], P(('groups', 'tile')), parts along dimension 0, may hold values from -6 to 6
- trial: bfloat16 [512, 256], replicated, may hold values from -0.375 to 0.375
- chol: bfloat16 [496, 2048, 256], P('tile'), may hold values from -0.01171875 to 0.01171875
- pattern: int32 [256], replicated, may hold values from 0 to 1023, as said below
- owner_counts: int32 [16], replicated, may hold values from 1 to 31, as said below
- chol_group: int32 [2048], replicated, may hold values from 0 to 3
- group_weight: float32 [4], replicated, may hold values from 0.5 to 2
- aux: int32 [32, 2048], P('groups'), parts along dimension 0, may hold values from -524288 to 524287
Outputs:
- advanced: bfloat16 [32, 512, 256], P(('groups', 'tile')), parts along dimension 0
- log_weight: float32 [32], P(('groups', 'tile')), parts along dimension 0
There are 2 independent parts, one for each index of `groups`. A program takes and returns all parts, laid end to end along the dimension named above; an argument that names none is the same for every part. Nothing has to cross between parts.
Inputs may be any that keep to these rules, and one draw needn't show every extreme that they name: `pattern`: values are distinct. Owners d and d + 8 together hold 32 tiles; slots of owner d past owner_counts[d] hold no tile.
All inputs are finite; a program needn't handle non-finite values.
Results may differ from a plain program's by a relative error of at most 0.009.
Values may be sent and summed in bfloat16 or wider, within the bound.
A program may use at most 128 MiB of HBM per device.

v0:
```python
import functools

import jax
import jax.numpy as jnp
from jax import lax
from jax.experimental import pallas as pl
from jax.experimental.pallas import tpu as pltpu
from jax.sharding import PartitionSpec as P

NBLK = 32
BF = jnp.bfloat16
F32 = jnp.float32
NT_DIMS = (((1,), (1,)), ((), ()))


def quot(x, k):
    if k & (k - 1) == 0:
        return lax.shift_right_logical(x, jnp.int32(k.bit_length() - 1))
    return lax.div(x, jnp.int32(k))


def mod(x, k):
    if k & (k - 1) == 0:
        return lax.bitwise_and(x, jnp.int32(k - 1))
    return lax.rem(x, jnp.int32(k))


def iota(shape, dim):
    return lax.broadcasted_iota(jnp.int32, shape, dim)


def hot(cond):
    return jnp.where(cond, 1.0, 0.0).astype(BF)


def dot(a, b):
    return jnp.dot(a, b, preferred_element_type=F32)


def swap_matrix(outer, inner):
    size = outer * inner
    row = iota((size, size), 0)
    col = iota((size, size), 1)
    return hot(col == mod(row, inner) * outer + quot(row, inner))


def kernel(
    n, cap, part_size, halves, chunk, gstep,
    walk_ref, factor_ref, trial_ref, chol_ref, pattern_ref, counts_ref, cgroup_ref, gweight_ref,
    aux_ref,
    adv_ref, lw_ref,
    chol_v, spots, green_v, sent, got, tiles_v, bias_acc, part, part_got, field_own, field_got,
    field_all, logw_own, logw_got, pot_acc, pot_v, back, back_got, v_mat,
    chol_sem, a_send, a_recv, r_send, r_recv, f_send, f_recv, l_send, l_recv, b_send, b_recv,
):
    me = lax.axis_index("tile")
    orbitals = walk_ref.shape[1]
    nchol, entries = chol_ref.shape[1], chol_ref.shape[2]
    ntile = pattern_ref.shape[1]
    wall = aux_ref.shape[0]
    side = orbitals // NBLK
    group = chunk // side
    ngroup = NBLK // group
    half = nchol // halves
    nch = half // chunk
    wrows = wall * nch // n
    parts = -(-cap // part_size)
    rows = n * part_size
    mine_k = lax.rem(me, nch)
    others = [lax.rem(me + off, n) for off in range(1, n)]

    def send(src, dst, ssem, rsem, dev):
        return pltpu.make_async_remote_copy(
            src_ref=src, dst_ref=dst, send_sem=ssem, recv_sem=rsem,
            device_id={"tile": dev}, device_id_type=pl.DeviceIdType.MESH,
        )

    barrier = pltpu.get_barrier_semaphore()
    for dst in others:
        pl.semaphore_signal(
            barrier, inc=1, device_id={"tile": dst}, device_id_type=pl.DeviceIdType.MESH
        )
    span = [(jp * part_size, min(cap, (jp + 1) * part_size)) for jp in range(parts)]
    chol_copies = {}
    for jp, (j0, j1) in enumerate(span):
        for h in range(halves):
            piece = (pl.ds(j0, j1 - j0), pl.ds(h * half, half), slice(None))
            chol_copies[jp, h] = pltpu.make_async_copy(
                chol_ref.at[piece], chol_v.at[piece], chol_sem.at[jp, h]
            )
            chol_copies[jp, h].start()

    perm = swap_matrix(side, NBLK)
    factor = dot(perm, factor_ref[0]).astype(BF)
    green = lax.dot_general(
        factor, trial_ref[...], NT_DIMS, preferred_element_type=F32
    ).astype(BF)
    for p in range(side):
        for c in range(ngroup):
            green_v[c * NBLK : (c + 1) * NBLK, p * chunk : (p + 1) * chunk] = green[
                p * NBLK : (p + 1) * NBLK, c * chunk : (c + 1) * chunk
            ]
    pat_row = pattern_ref[...]
    pat_col = jnp.transpose(jnp.broadcast_to(pat_row, (128, ntile)))[:, :1]

    def place(pat):
        return quot(mod(pat, NBLK), group) * NBLK + quot(pat, NBLK)

    pick = hot(place(pat_col) == iota((ntile, ngroup * NBLK), 1))
    put = hot(place(pat_row) == iota((ngroup * NBLK, ntile), 0))
    col_mask = hot(mod(pat_col, group) == quot(iota((ntile, chunk), 1), side))
    col_mask = jnp.concatenate([col_mask] * side, axis=1)
    wide_lane = iota((entries, side * chunk), 1)
    spots[...] = hot(
        iota((entries, side * chunk), 0) == quot(wide_lane, chunk) * side + mod(wide_lane, side)
    )
    chosen = dot(pick, green_v[...]).astype(BF) * col_mask
    green_t = lax.dot_general(chosen, spots[...], NT_DIMS, preferred_element_type=F32).astype(BF)

    first = jnp.int32(0)
    lane = iota((1, rows), 1)
    slot = iota((part_size, ntile), 0)
    tile_lane = iota((part_size, ntile), 1)
    lane_tile = [jnp.full((1, rows), -1, jnp.int32) for _ in range(parts)]
    own = [[] for _ in range(parts)]
    for d in range(n):
        held = counts_ref[d]
        for jp in range(parts):
            at = slot + jp * part_size
            own[jp].append(jnp.where((tile_lane == at + first) & (at < held), 1.0, 0.0))
            in_part = lane - d * part_size
            at = in_part + jp * part_size
            live = (in_part >= 0) & (in_part < part_size) & (at < held)
            lane_tile[jp] = jnp.where(live, at + first, lane_tile[jp])
        first = first + held

    a_copies = [[] for _ in range(parts)]
    for jp in range(parts):
        rows_out = dot(jnp.concatenate(own[jp], axis=0).astype(BF), green_t)
        sent[jp] = rows_out.astype(BF).reshape(n, part_size, entries)
        if jp == 0:
            pl.semaphore_wait(barrier, n - 1)
        for i, dst in enumerate(others):
            copy = send(
                sent.at[jp, dst], got.at[jp, me], a_send.at[jp, i], a_recv.at[jp, i], dst
            )
            copy.start()
            a_copies[jp].append(copy)
        got[jp, me] = sent[jp, me]

    r_copies, f_copies, l_copies = [], [[] for _ in range(halves)], []
    logw_parts = []

    def bias_block(jp, h, g):
        j0, j1 = span[jp]
        g0 = h * half + g * gstep
        total = bias_acc[:, g0 : g0 + gstep] if jp else jnp.zeros((wall, gstep), F32)
        for j in range(j0, j1):
            total = total + lax.dot_general(
                tiles_v[j], chol_v[j, g0 : g0 + gstep, :], NT_DIMS, preferred_element_type=F32
            )
        if jp < parts - 1:
            bias_acc[:, g0 : g0 + gstep] = total
            return
        for k in range(gstep // chunk):
            kk = g * (gstep // chunk) + k
            part[h, kk] = total[:, k * chunk : (k + 1) * chunk]
            for wg in range(n // nch):
                d = wg * nch + kk
                copy = send(
                    part.at[h, kk, wg * wrows : (wg + 1) * wrows], part_got.at[h, me],
                    r_send.at[h, d], r_recv.at[h, me], d,
                )
                r_copies.append((d, copy))
                pl.when(me != d)(copy.start)

                @pl.when(me == d)
                def _():
                    part_got[h, me] = part[h, kk, wg * wrows : (wg + 1) * wrows]

    def reduce_bias(h):
        for src in others:
            send(
                part.at[h, 0, 0:wrows], part_got.at[h, src], r_send.at[h, src],
                r_recv.at[h, src], src,
            ).wait_recv()
        bias = part_got[h, 0]
        for s in range(1, n):
            bias = bias + part_got[h, s]
        drawn = jnp.zeros((wrows, chunk), jnp.int32)
        kind = jnp.zeros((1, chunk), jnp.int32)
        for d in range(n):
            g0 = h * half + (d % nch) * chunk
            w0 = (d // nch) * wrows
            drawn = jnp.where(me == d, aux_ref[w0 : w0 + wrows, g0 : g0 + chunk], drawn)
            kind = jnp.where(me == d, cgroup_ref[:, g0 : g0 + chunk], kind)
        weight = jnp.zeros((1, chunk), F32)
        for k in range(gweight_ref.shape[0]):
            weight = jnp.where(kind == k, gweight_ref[k], weight)
        sampled = drawn.astype(F32) * (1.0 / 262144.0)
        field_own[h] = (weight * (sampled - bias)).astype(BF).astype(F32)
        for i, dst in enumerate(others):
            copy = send(
                field_own.at[h], field_got.at[h, me], f_send.at[h, i], f_recv.at[h, i], dst
            )
            copy.start()
            f_copies[h].append(copy)
        field_got[h, me] = field_own[h]
        logw_parts.append(
            jnp.sum(sampled * bias - 0.5 * bias * bias, axis=1, keepdims=True)
        )

    def gather_fields(h):
        for copy in f_copies[h]:
            copy.wait_recv()
        for s in range(n):
            g0 = h * half + (s % nch) * chunk
            w0 = (s // nch) * wrows
            field_all[w0 : w0 + wrows, g0 : g0 + chunk] = field_got[h, s]
        return field_all[:, h * half : (h + 1) * half].astype(BF)

    blocks = half // gstep
    for jp in range(parts):
        for copy in a_copies[jp]:
            copy.wait_recv()
        j0 = jp * part_size
        tiles_v[j0 : j0 + part_size] = dot(
            swap_matrix(part_size, wall), got[jp].reshape(rows, entries)
        ).astype(BF).reshape(part_size, wall, entries)
        for h in range(halves):
            chol_copies[jp, h].wait()
            for g in range(blocks):
                if jp == parts - 1 and h > 0 and g == blocks - 1:
                    reduce_bias(h - 1)
                bias_block(jp, h, g)

    fields = gather_fields(0)
    for h in range(halves - 1):
        for jp, (j0, j1) in enumerate(span):
            for j in range(j0, j1):
                new = dot(fields, chol_v[j, h * half : (h + 1) * half, :])
                pot_acc[j] = new if h == 0 else pot_acc[j] + new
            if jp == 0 and h == halves - 2:
                reduce_bias(halves - 1)
        fields = gather_fields(h + 1)
    b_copies = [[] for _ in range(parts)]
    h = halves - 1
    for jp, (j0, j1) in enumerate(span):
        for j in range(j0, j1):
            pot_v[j] = (
                pot_acc[j] + dot(fields, chol_v[j, h * half : (h + 1) * half, :])
            ).astype(BF)
        for j in range(j1, j0 + part_size):
            pot_v[j] = jnp.zeros((wall, entries), BF)
        back[jp] = dot(
            swap_matrix(wall, part_size), pot_v[j0 : j0 + part_size].reshape(rows, entries)
        ).astype(BF).reshape(n, part_size, entries)
        for i, dst in enumerate(others):
            copy = send(
                back.at[jp, dst], back_got.at[jp, me], b_send.at[jp, i], b_recv.at[jp, i], dst
            )
            copy.start()
            b_copies[jp].append(copy)
        back_got[jp, me] = back[jp, me]

    logw = sum(logw_parts[1:], logw_parts[0])
    logw_own[...] = jnp.broadcast_to(logw, logw_own.shape)
    for off in range(1, nch):
        dst = me - mine_k + lax.rem(mine_k + off, nch)
        copy = send(logw_own, logw_got.at[mine_k], l_send.at[off], l_recv.at[off], dst)
        copy.start()
        l_copies.append(copy)
    logw_got[mine_k] = logw_own[...]
    unperm = swap_matrix(NBLK, side)
    gather = [hot(iota((ntile, rows), 0) == lane_tile[jp]) for jp in range(parts)]

    pot_t = jnp.zeros((ntile, entries), F32)
    for jp in range(parts):
        for copy in b_copies[jp]:
            copy.wait_recv()
        pot_t = pot_t + dot(gather[jp], back_got[jp].reshape(rows, entries))
    wide = dot(pot_t.astype(BF), spots[...]).astype(BF) * col_mask
    placed = dot(put, wide).astype(BF)
    for p in range(side):
        for c in range(ngroup):
            v_mat[p * NBLK : (p + 1) * NBLK, c * chunk : (c + 1) * chunk] = placed[
                c * NBLK : (c + 1) * NBLK, p * chunk : (p + 1) * chunk
            ]
    v_mat[...] = dot(unperm, v_mat[...]).astype(BF)
    term = walk_ref[0]
    running = term.astype(F32)
    for degree in range(1, 5):
        term = (dot(v_mat[...], term) / degree).astype(BF)
        running = running + term.astype(F32)
    adv_ref[0] = running.astype(BF)

    for copy in l_copies:
        copy.wait_recv()
    logw = logw_got[0]
    for s in range(1, nch):
        logw = logw + logw_got[s]
    mine = (iota(logw.shape, 0) == lax.rem(me, wrows)) & (iota(logw.shape, 1) == 0)
    lw_ref[0] = jnp.sum(jnp.where(mine, logw, 0.0))
    for copy in sum(a_copies + f_copies + b_copies, l_copies):
        copy.wait_send()
    for d, copy in r_copies:
        pl.when(me != d)(copy.wait_send)


def per_device(
    walkers, green_factor, trial, chol, pattern, owner_counts, chol_group, group_weight, aux
):
    n = owner_counts.shape[0]
    cap, nchol, entries = chol.shape
    wall = aux.shape[0]
    assert walkers.shape[0] == 1 and wall == n
    orbitals = walkers.shape[1]
    chunk, part_size, halves, gstep = 128, 16, 2, 256
    nch = nchol // halves // chunk
    assert n % nch == 0
    parts = -(-cap // part_size)
    side = orbitals // NBLK
    wrows = wall * nch // n
    dma = pltpu.SemaphoreType.DMA
    vmem = pl.BlockSpec(memory_space=pltpu.VMEM)
    smem = pl.BlockSpec(memory_space=pltpu.SMEM)
    advanced, log_weight = pl.pallas_call(
        functools.partial(kernel, n, cap, part_size, halves, chunk, gstep),
        out_shape=(
            jax.ShapeDtypeStruct(walkers.shape, BF),
            jax.ShapeDtypeStruct((1,), F32),
        ),
        in_specs=[vmem, vmem, vmem, pl.BlockSpec(memory_space=pl.ANY), vmem, smem, vmem, smem, vmem],
        out_specs=(vmem, smem),
        scratch_shapes=[
            pltpu.VMEM((cap, nchol, entries), BF),
            pltpu.VMEM((entries, side * chunk), BF),
            pltpu.VMEM((orbitals // chunk * NBLK, side * chunk), BF),
            pltpu.VMEM((parts, n, part_size, entries), BF),
            pltpu.VMEM((parts, n, part_size, entries), BF),
            pltpu.VMEM((parts * part_size, wall, entries), BF),
            pltpu.VMEM((wall, nchol), F32),
            pltpu.VMEM((halves, nch, wall, chunk), F32),
            pltpu.VMEM((halves, n, wrows, chunk), F32),
            pltpu.VMEM((halves, wrows, chunk), F32),
            pltpu.VMEM((halves, n, wrows, chunk), F32),
            pltpu.VMEM((wall, nchol), F32),
            pltpu.VMEM((wrows, chunk), F32),
            pltpu.VMEM((nch, wrows, chunk), F32),
            pltpu.VMEM((cap, wall, entries), F32),
            pltpu.VMEM((parts * part_size, wall, entries), BF),
            pltpu.VMEM((parts, n, part_size, entries), BF),
            pltpu.VMEM((parts, n, part_size, entries), BF),
            pltpu.VMEM((orbitals, orbitals), BF),
            dma((parts, halves)),
            dma((parts, n)), dma((parts, n)),
            dma((halves, n)), dma((halves, n)),
            dma((halves, n)), dma((halves, n)),
            dma((nch,)), dma((nch,)),
            dma((parts, n)), dma((parts, n)),
        ],
        compiler_params=pltpu.CompilerParams(
            collective_id=0, has_side_effects=True, vmem_limit_bytes=56 * 2**20
        ),
        cost_estimate=pl.CostEstimate(
            flops=4 * wall * cap * nchol * entries, bytes_accessed=2 * chol.size, transcendentals=0
        ),
    )(
        walkers, green_factor, trial, chol, pattern.reshape(1, -1), owner_counts,
        chol_group.reshape(1, -1), group_weight, aux,
    )
    return advanced, log_weight


def solution(mesh):
    return jax.shard_map(
        per_device,
        mesh=mesh,
        in_specs=(
            P(("groups", "tile"), None, None),
            P(("groups", "tile"), None, None),
            P(),
            P("tile", None, None),
            P(),
            P(),
            P(),
            P(),
            P("groups", None),
        ),
        out_specs=(P(("groups", "tile"), None, None), P(("groups", "tile"))),
        check_vma=False,
    )
```

profile of v0, /device:TPU:0, one launch (start us, length us, event | category | flops | bytes accessed | tf_op | source)
XLA Modules:
  0.0 54.6 jit_solution(10625487377569182805)
XLA Ops:
  0.6 50.5 %shard_map.104 = (bf16[1,512,256]{2,1,0:T(8,128)(2,1)}, f32[1]{0:T(128)}) custom-call(bf16[1,512,256]{2,1,0:T(8,128)(2,1)} %walk_ref.1, bf16[1,512,256]{2,1,0:T(8,128)(2,1)} %factor_ref.1, bf16[512,256]{1,0:T(8,128)(2,1)} %trial_ref.1, bf16[31,2048,256]{2,1,0:T(8,128)(2,1)} %chol_ref.1, s32[1,256]{1,0:T(1,128)} %bitcast.3, s32[16]{0:T(128)} %counts_ref.1, ...), custom_call_target="tpu_custom_call" | custom-call | flops 1040187392 | bytes 32505856 | tf_op jit(solution)/shard_map/pallas_call | solution.py:327
  51.1 1.7 %copy.13 = bf16[1,512,256]{2,1,0:T(8,128)(2,1)} copy(bf16[1,512,256]{2,1,0:T(8,128)(2,1)} %get-tuple-element.4) | data formatting | bytes 524288
where the time goes:
time: 54.8 us; the launch traced here: 54.6 us
  Pallas kernels  50.5 us (92%)
  between operations  2.41 us (4%)
  local copies, waits for them, and re-layouts  1.67 us (3%)
    pallas_call x1, Pallas kernels, per_device(): pl.pallas_call(functools.partial(kernel, n, cap, part_size, halves, chunk...  50.5 us
    unnamed x1, local copies, waits for them, and re-layouts  1.67 us

commit v1 on v0

--- a/solution.py
+++ b/solution.py
@@ -45,7 +45,7 @@
 
 
 def kernel(
-    n, cap, part_size, halves, chunk, gstep,
+    n, cap, part_size, halves, chunk,
     walk_ref, factor_ref, trial_ref, chol_ref, pattern_ref, counts_ref, cgroup_ref, gweight_ref,
     aux_ref,
     adv_ref, lw_ref,
@@ -151,20 +151,20 @@
     r_copies, f_copies, l_copies = [], [[] for _ in range(halves)], []
     logw_parts = []
 
-    def bias_block(jp, h, g):
+    def bias_half(jp, h):
         j0, j1 = span[jp]
-        g0 = h * half + g * gstep
-        total = bias_acc[:, g0 : g0 + gstep] if jp else jnp.zeros((wall, gstep), F32)
+        g0 = h * half
         for j in range(j0, j1):
-            total = total + lax.dot_general(
-                tiles_v[j], chol_v[j, g0 : g0 + gstep, :], NT_DIMS, preferred_element_type=F32
-            )
+            new = lax.dot_general(
+                chol_v[j, g0 : g0 + half, :], tiles_v[j], NT_DIMS, preferred_element_type=F32
+            )
+            bias_acc[g0 : g0 + half, :] = bias_acc[g0 : g0 + half, :] + new if j else new
         if jp < parts - 1:
-            bias_acc[:, g0 : g0 + gstep] = total
             return
-        for k in range(gstep // chunk):
-            kk = g * (gstep // chunk) + k
-            part[h, kk] = total[:, k * chunk : (k + 1) * chunk]
+        for kk in range(nch):
+            part[h, kk] = jnp.transpose(
+                bias_acc[g0 + kk * chunk : g0 + (kk + 1) * chunk, :]
+            )
             for wg in range(n // nch):
                 d = wg * nch + kk
                 copy = send(
@@ -219,7 +219,6 @@
             field_all[w0 : w0 + wrows, g0 : g0 + chunk] = field_got[h, s]
         return field_all[:, h * half : (h + 1) * half].astype(BF)
 
-    blocks = half // gstep
     for jp in range(parts):
         for copy in a_copies[jp]:
             copy.wait_recv()
@@ -229,10 +228,9 @@
         ).astype(BF).reshape(part_size, wall, entries)
         for h in range(halves):
             chol_copies[jp, h].wait()
-            for g in range(blocks):
-                if jp == parts - 1 and h > 0 and g == blocks - 1:
-                    reduce_bias(h - 1)
-                bias_block(jp, h, g)
+            bias_half(jp, h)
+            if jp == parts - 1 and h > 0:
+                reduce_bias(h - 1)
 
     fields = gather_fields(0)
     for h in range(halves - 1):
@@ -315,7 +313,7 @@
     wall = aux.shape[0]
     assert walkers.shape[0] == 1 and wall == n
     orbitals = walkers.shape[1]
-    chunk, part_size, halves, gstep = 128, 16, 2, 256
+    chunk, part_size, halves = 128, 16, 2
     nch = nchol // halves // chunk
     assert n % nch == 0
     parts = -(-cap // part_size)
@@ -325,7 +323,7 @@
     vmem = pl.BlockSpec(memory_space=pltpu.VMEM)
     smem = pl.BlockSpec(memory_space=pltpu.SMEM)
     advanced, log_weight = pl.pallas_call(
-        functools.partial(kernel, n, cap, part_size, halves, chunk, gstep),
+        functools.partial(kernel, n, cap, part_size, halves, chunk),
         out_shape=(
             jax.ShapeDtypeStruct(walkers.shape, BF),
             jax.ShapeDtypeStruct((1,), F32),
@@ -339,7 +337,7 @@
             pltpu.VMEM((parts, n, part_size, entries), BF),
             pltpu.VMEM((parts, n, part_size, entries), BF),
             pltpu.VMEM((parts * part_size, wall, entries), BF),
-            pltpu.VMEM((wall, nchol), F32),
+            pltpu.VMEM((nchol, wall), F32),
             pltpu.VMEM((halves, nch, wall, chunk), F32),
             pltpu.VMEM((halves, n, wrows, chunk), F32),
             pltpu.VMEM((halves, wrows, chunk), F32),

time: 54.8 us -> 55.7 us (1.016)
  Pallas kernels: 50.5 us -> 51.4 us
    pallas_call x1, Pallas kernels: 50.5 us -> 51.4 us  [per_device(): pl.pallas_call(functools.partial(kernel, n, cap, part_size, halves, chunk...]
where the time goes in v1:
time: 55.7 us; the launch traced here: 55.5 us
  Pallas kernels  51.4 us (92%)
  between operations  2.41 us (4%)
  local copies, waits for them, and re-layouts  1.67 us (3%)
    pallas_call x1, Pallas kernels, per_device(): pl.pallas_call(functools.partial(kernel, n, cap, part_size, halves, chunk...  51.4 us
    unnamed x1, local copies, waits for them, and re-layouts  1.67 us

profile of v1, /device:TPU:0, one launch (start us, length us, event | category | flops | bytes accessed | tf_op | source)
XLA Modules:
  0.0 55.5 jit_solution(9138219071779960028)
XLA Ops:
  0.6 51.4 %shard_map.104 = (bf16[1,512,256]{2,1,0:T(8,128)(2,1)}, f32[1]{0:T(128)}) custom-call(bf16[1,512,256]{2,1,0:T(8,128)(2,1)} %walk_ref.1, bf16[1,512,256]{2,1,0:T(8,128)(2,1)} %factor_ref.1, bf16[512,256]{1,0:T(8,128)(2,1)} %trial_ref.1, bf16[31,2048,256]{2,1,0:T(8,128)(2,1)} %chol_ref.1, s32[1,256]{1,0:T(1,128)} %bitcast.3, s32[16]{0:T(128)} %counts_ref.1, ...), custom_call_target="tpu_custom_call" | custom-call | flops 1040187392 | bytes 32505856 | tf_op jit(solution)/shard_map/pallas_call | solution.py:325
  52.0 1.7 %copy.13 = bf16[1,512,256]{2,1,0:T(8,128)(2,1)} copy(bf16[1,512,256]{2,1,0:T(8,128)(2,1)} %get-tuple-element.4) | data formatting | bytes 524288

commit v2 on v1

--- a/solution.py
+++ b/solution.py
@@ -50,7 +50,7 @@
     aux_ref,
     adv_ref, lw_ref,
     chol_v, spots, green_v, sent, got, tiles_v, bias_acc, part, part_got, field_own, field_got,
-    field_all, logw_own, logw_got, pot_acc, pot_v, back, back_got, v_mat,
+    field_all, fields_v, logw_own, logw_got, pot_acc, pot_v, back, back_got, v_mat, term_v, running_v,
     chol_sem, a_send, a_recv, r_send, r_recv, f_send, f_recv, l_send, l_recv, b_send, b_recv,
 ):
     me = lax.axis_index("tile")
@@ -151,20 +151,34 @@
     r_copies, f_copies, l_copies = [], [[] for _ in range(halves)], []
     logw_parts = []
 
-    def bias_half(jp, h):
+    def over_tiles(j0, j1, body, carry):
+        step = max(u for u in range(1, 8) if (j1 - j0) % u == 0)
+
+        def several(i, carry):
+            for u in range(step):
+                carry = body(j0 + i * step + u, carry)
+            return carry
+
+        return lax.fori_loop(0, (j1 - j0) // step, several, carry)
+
+    def bias_block(jp, h, g0, size):
         j0, j1 = span[jp]
-        g0 = h * half
-        for j in range(j0, j1):
-            new = lax.dot_general(
-                chol_v[j, g0 : g0 + half, :], tiles_v[j], NT_DIMS, preferred_element_type=F32
+        start = h * half + g0
+
+        def add(j, total):
+            return total + lax.dot_general(
+                tiles_v[j], chol_v[j, start : start + size, :], NT_DIMS,
+                preferred_element_type=F32,
             )
-            bias_acc[g0 : g0 + half, :] = bias_acc[g0 : g0 + half, :] + new if j else new
+
+        total = bias_acc[:, start : start + size] if jp else jnp.zeros((wall, size), F32)
+        total = over_tiles(j0, j1, add, total)
         if jp < parts - 1:
+            bias_acc[:, start : start + size] = total
             return
-        for kk in range(nch):
-            part[h, kk] = jnp.transpose(
-                bias_acc[g0 + kk * chunk : g0 + (kk + 1) * chunk, :]
-            )
+        for k in range(size // chunk):
+            kk = g0 // chunk + k
+            part[h, kk] = total[:, k * chunk : (k + 1) * chunk]
             for wg in range(n // nch):
                 d = wg * nch + kk
                 copy = send(
@@ -217,7 +231,7 @@
             g0 = h * half + (s % nch) * chunk
             w0 = (s // nch) * wrows
             field_all[w0 : w0 + wrows, g0 : g0 + chunk] = field_got[h, s]
-        return field_all[:, h * half : (h + 1) * half].astype(BF)
+        fields_v[h] = field_all[:, h * half : (h + 1) * half].astype(BF)
 
     for jp in range(parts):
         for copy in a_copies[jp]:
@@ -228,26 +242,35 @@
         ).astype(BF).reshape(part_size, wall, entries)
         for h in range(halves):
             chol_copies[jp, h].wait()
-            bias_half(jp, h)
             if jp == parts - 1 and h > 0:
+                bias_block(jp, h, 0, half // 2)
                 reduce_bias(h - 1)
-
-    fields = gather_fields(0)
+                bias_block(jp, h, half // 2, half // 2)
+            else:
+                bias_block(jp, h, 0, half)
+
+    gather_fields(0)
     for h in range(halves - 1):
         for jp, (j0, j1) in enumerate(span):
-            for j in range(j0, j1):
-                new = dot(fields, chol_v[j, h * half : (h + 1) * half, :])
+            def spread(j, carry):
+                new = dot(fields_v[h], chol_v[j, h * half : (h + 1) * half, :])
                 pot_acc[j] = new if h == 0 else pot_acc[j] + new
+                return carry
+
+            over_tiles(j0, j1, spread, 0)
             if jp == 0 and h == halves - 2:
                 reduce_bias(halves - 1)
-        fields = gather_fields(h + 1)
+        gather_fields(h + 1)
     b_copies = [[] for _ in range(parts)]
     h = halves - 1
     for jp, (j0, j1) in enumerate(span):
-        for j in range(j0, j1):
+        def finish(j, carry):
             pot_v[j] = (
-                pot_acc[j] + dot(fields, chol_v[j, h * half : (h + 1) * half, :])
+                pot_acc[j] + dot(fields_v[h], chol_v[j, h * half : (h + 1) * half, :])
             ).astype(BF)
+            return carry
+
+        over_tiles(j0, j1, finish, 0)
         for j in range(j1, j0 + part_size):
             pot_v[j] = jnp.zeros((wall, entries), BF)
         back[jp] = dot(
@@ -285,12 +308,17 @@
                 c * NBLK : (c + 1) * NBLK, p * chunk : (p + 1) * chunk
             ]
     v_mat[...] = dot(unperm, v_mat[...]).astype(BF)
-    term = walk_ref[0]
-    running = term.astype(F32)
-    for degree in range(1, 5):
-        term = (dot(v_mat[...], term) / degree).astype(BF)
-        running = running + term.astype(F32)
-    adv_ref[0] = running.astype(BF)
+    term_v[...] = walk_ref[0]
+    running_v[...] = walk_ref[0].astype(F32)
+
+    def taylor(degree, carry):
+        term = (dot(v_mat[...], term_v[...]) / degree.astype(F32)).astype(BF)
+        term_v[...] = term
+        running_v[...] = running_v[...] + term.astype(F32)
+        return carry
+
+    lax.fori_loop(1, 5, taylor, 0)
+    adv_ref[0] = running_v[...].astype(BF)
 
     for copy in l_copies:
         copy.wait_recv()
@@ -337,12 +365,13 @@
             pltpu.VMEM((parts, n, part_size, entries), BF),
             pltpu.VMEM((parts, n, part_size, entries), BF),
             pltpu.VMEM((parts * part_size, wall, entries), BF),
-            pltpu.VMEM((nchol, wall), F32),
+            pltpu.VMEM((wall, nchol), F32),
             pltpu.VMEM((halves, nch, wall, chunk), F32),
             pltpu.VMEM((halves, n, wrows, chunk), F32),
             pltpu.VMEM((halves, wrows, chunk), F32),
             pltpu.VMEM((halves, n, wrows, chunk), F32),
             pltpu.VMEM((wall, nchol), F32),
+            pltpu.VMEM((halves, wall, nchol // halves), BF),
             pltpu.VMEM((wrows, chunk), F32),
             pltpu.VMEM((nch, wrows, chunk), F32),
             pltpu.VMEM((cap, wall, entries), F32),
@@ -350,6 +379,8 @@
             pltpu.VMEM((parts, n, part_size, entries), BF),
             pltpu.VMEM((parts, n, part_size, entries), BF),
             pltpu.VMEM((orbitals, orbitals), BF),
+            pltpu.VMEM(walkers.shape[1:], BF),
+            pltpu.VMEM(walkers.shape[1:], F32),
             dma((parts, halves)),
             dma((parts, n)), dma((parts, n)),
             dma((halves, n)), dma((halves, n)),

time: 55.7 us -> 53.6 us (0.962)
  Pallas kernels: 51.4 us -> 49.3 us
    pallas_call x1, Pallas kernels: 51.4 us -> 49.3 us  [per_device(): pl.pallas_call(functools.partial(kernel, n, cap, part_size, halves, chunk...]
where the time goes in v2:
time: 53.6 us; the launch traced here: 53.4 us
  Pallas kernels  49.3 us (92%)
  between operations  2.41 us (4%)
  local copies, waits for them, and re-layouts  1.67 us (3%)
    pallas_call x1, Pallas kernels, per_device(): pl.pallas_call(functools.partial(kernel, n, cap, part_size, halves, chunk...  49.3 us
    unnamed x1, local copies, waits for them, and re-layouts  1.67 us

profile of v2, /device:TPU:0, one launch (start us, length us, event | category | flops | bytes accessed | tf_op | source)
XLA Modules:
  0.0 53.4 jit_solution(15843000566005442737)
XLA Ops:
  0.6 49.3 %shard_map.104 = (bf16[1,512,256]{2,1,0:T(8,128)(2,1)}, f32[1]{0:T(128)}) custom-call(bf16[1,512,256]{2,1,0:T(8,128)(2,1)} %walk_ref.1, bf16[1,512,256]{2,1,0:T(8,128)(2,1)} %factor_ref.1, bf16[512,256]{1,0:T(8,128)(2,1)} %trial_ref.1, bf16[31,2048,256]{2,1,0:T(8,128)(2,1)} %chol_ref.1, s32[1,256]{1,0:T(1,128)} %bitcast.3, s32[16]{0:T(128)} %counts_ref.1, ...), custom_call_target="tpu_custom_call" | custom-call | flops 1040187392 | bytes 32505856 | tf_op jit(solution)/shard_map/pallas_call | solution.py:353
  50.0 1.7 %copy.13 = bf16[1,512,256]{2,1,0:T(8,128)(2,1)} copy(bf16[1,512,256]{2,1,0:T(8,128)(2,1)} %get-tuple-element.4) | data formatting | bytes 524288

commit v3 on v2

--- a/solution.py
+++ b/solution.py
@@ -75,6 +75,12 @@
             device_id={"tile": dev}, device_id_type=pl.DeviceIdType.MESH,
         )
 
+    def received(ref, sem):
+        send(ref, ref, sem, sem, others[0]).wait_recv()
+
+    def sent_out(ref, sem):
+        send(ref, ref, sem, sem, others[0]).wait_send()
+
     barrier = pltpu.get_barrier_semaphore()
     for dst in others:
         pl.semaphore_signal(
@@ -88,7 +94,8 @@
             chol_copies[jp, h] = pltpu.make_async_copy(
                 chol_ref.at[piece], chol_v.at[piece], chol_sem.at[jp, h]
             )
-            chol_copies[jp, h].start()
+            if jp == 0:
+                chol_copies[jp, h].start()
 
     perm = swap_matrix(side, NBLK)
     factor = dot(perm, factor_ref[0]).astype(BF)
@@ -134,21 +141,18 @@
             lane_tile[jp] = jnp.where(live, at + first, lane_tile[jp])
         first = first + held
 
-    a_copies = [[] for _ in range(parts)]
     for jp in range(parts):
         rows_out = dot(jnp.concatenate(own[jp], axis=0).astype(BF), green_t)
         sent[jp] = rows_out.astype(BF).reshape(n, part_size, entries)
         if jp == 0:
             pl.semaphore_wait(barrier, n - 1)
-        for i, dst in enumerate(others):
-            copy = send(
-                sent.at[jp, dst], got.at[jp, me], a_send.at[jp, i], a_recv.at[jp, i], dst
-            )
-            copy.start()
-            a_copies[jp].append(copy)
+        for dst in others:
+            send(sent.at[jp, dst], got.at[jp, me], a_send.at[jp], a_recv.at[jp], dst).start()
+        if jp + 1 < parts:
+            for h in range(halves):
+                chol_copies[jp + 1, h].start()
         got[jp, me] = sent[jp, me]
 
-    r_copies, f_copies, l_copies = [], [[] for _ in range(halves)], []
     logw_parts = []
 
     def over_tiles(j0, j1, body, carry):
@@ -177,27 +181,19 @@
             bias_acc[:, start : start + size] = total
             return
         for k in range(size // chunk):
-            kk = g0 // chunk + k
-            part[h, kk] = total[:, k * chunk : (k + 1) * chunk]
             for wg in range(n // nch):
-                d = wg * nch + kk
-                copy = send(
-                    part.at[h, kk, wg * wrows : (wg + 1) * wrows], part_got.at[h, me],
-                    r_send.at[h, d], r_recv.at[h, me], d,
-                )
-                r_copies.append((d, copy))
-                pl.when(me != d)(copy.start)
-
-                @pl.when(me == d)
-                def _():
-                    part_got[h, me] = part[h, kk, wg * wrows : (wg + 1) * wrows]
+                part[h, wg * nch + g0 // chunk + k] = total[
+                    wg * wrows : (wg + 1) * wrows, k * chunk : (k + 1) * chunk
+                ]
+        if g0 + size == half:
+            for dst in others:
+                send(
+                    part.at[h, dst], part_got.at[h, me], r_send.at[h], r_recv.at[h], dst
+                ).start()
+            part_got[h, me] = part[h, me]
 
     def reduce_bias(h):
-        for src in others:
-            send(
-                part.at[h, 0, 0:wrows], part_got.at[h, src], r_send.at[h, src],
-                r_recv.at[h, src], src,
-            ).wait_recv()
+        received(part_got.at[h, 0 : n - 1], r_recv.at[h])
         bias = part_got[h, 0]
         for s in range(1, n):
             bias = bias + part_got[h, s]
@@ -213,20 +209,17 @@
             weight = jnp.where(kind == k, gweight_ref[k], weight)
         sampled = drawn.astype(F32) * (1.0 / 262144.0)
         field_own[h] = (weight * (sampled - bias)).astype(BF).astype(F32)
-        for i, dst in enumerate(others):
-            copy = send(
-                field_own.at[h], field_got.at[h, me], f_send.at[h, i], f_recv.at[h, i], dst
-            )
-            copy.start()
-            f_copies[h].append(copy)
+        for dst in others:
+            send(
+                field_own.at[h], field_got.at[h, me], f_send.at[h], f_recv.at[h], dst
+            ).start()
         field_got[h, me] = field_own[h]
         logw_parts.append(
             jnp.sum(sampled * bias - 0.5 * bias * bias, axis=1, keepdims=True)
         )
 
     def gather_fields(h):
-        for copy in f_copies[h]:
-            copy.wait_recv()
+        received(field_got.at[h, 0 : n - 1], f_recv.at[h])
         for s in range(n):
             g0 = h * half + (s % nch) * chunk
             w0 = (s // nch) * wrows
@@ -234,8 +227,7 @@
         fields_v[h] = field_all[:, h * half : (h + 1) * half].astype(BF)
 
     for jp in range(parts):
-        for copy in a_copies[jp]:
-            copy.wait_recv()
+        received(got.at[jp, 0 : n - 1], a_recv.at[jp])
         j0 = jp * part_size
         tiles_v[j0 : j0 + part_size] = dot(
             swap_matrix(part_size, wall), got[jp].reshape(rows, entries)
@@ -261,7 +253,6 @@
             if jp == 0 and h == halves - 2:
                 reduce_bias(halves - 1)
         gather_fields(h + 1)
-    b_copies = [[] for _ in range(parts)]
     h = halves - 1
     for jp, (j0, j1) in enumerate(span):
         def finish(j, carry):
@@ -276,29 +267,30 @@
         back[jp] = dot(
             swap_matrix(wall, part_size), pot_v[j0 : j0 + part_size].reshape(rows, entries)
         ).astype(BF).reshape(n, part_size, entries)
-        for i, dst in enumerate(others):
-            copy = send(
-                back.at[jp, dst], back_got.at[jp, me], b_send.at[jp, i], b_recv.at[jp, i], dst
-            )
-            copy.start()
-            b_copies[jp].append(copy)
+        for dst in others:
+            send(
+                back.at[jp, dst], back_got.at[jp, me], b_send.at[jp], b_recv.at[jp], dst
+            ).start()
         back_got[jp, me] = back[jp, me]
 
     logw = sum(logw_parts[1:], logw_parts[0])
     logw_own[...] = jnp.broadcast_to(logw, logw_own.shape)
     for off in range(1, nch):
         dst = me - mine_k + lax.rem(mine_k + off, nch)
-        copy = send(logw_own, logw_got.at[mine_k], l_send.at[off], l_recv.at[off], dst)
-        copy.start()
-        l_copies.append(copy)
+        send(logw_own, logw_got.at[mine_k], l_send, l_recv, dst).start()
     logw_got[mine_k] = logw_own[...]
     unperm = swap_matrix(NBLK, side)
     gather = [hot(iota((ntile, rows), 0) == lane_tile[jp]) for jp in range(parts)]
 
+    for h in range(halves):
+        sent_out(part_got.at[h, 0 : n - 1], r_send.at[h])
+        sent_out(field_got.at[h, 0 : n - 1], f_send.at[h])
+    for jp in range(parts):
+        sent_out(got.at[jp, 0 : n - 1], a_send.at[jp])
+
     pot_t = jnp.zeros((ntile, entries), F32)
     for jp in range(parts):
-        for copy in b_copies[jp]:
-            copy.wait_recv()
+        received(back_got.at[jp, 0 : n - 1], b_recv.at[jp])
         pot_t = pot_t + dot(gather[jp], back_got[jp].reshape(rows, entries))
     wide = dot(pot_t.astype(BF), spots[...]).astype(BF) * col_mask
     placed = dot(put, wide).astype(BF)
@@ -320,17 +312,15 @@
     lax.fori_loop(1, 5, taylor, 0)
     adv_ref[0] = running_v[...].astype(BF)
 
-    for copy in l_copies:
-        copy.wait_recv()
+    received(logw_got.at[0 : nch - 1], l_recv)
     logw = logw_got[0]
     for s in range(1, nch):
         logw = logw + logw_got[s]
     mine = (iota(logw.shape, 0) == lax.rem(me, wrows)) & (iota(logw.shape, 1) == 0)
     lw_ref[0] = jnp.sum(jnp.where(mine, logw, 0.0))
-    for copy in sum(a_copies + f_copies + b_copies, l_copies):
-        copy.wait_send()
-    for d, copy in r_copies:
-        pl.when(me != d)(copy.wait_send)
+    sent_out(logw_got.at[0 : nch - 1], l_send)
+    for jp in range(parts):
+        sent_out(back_got.at[jp, 0 : n - 1], b_send.at[jp])
 
 
 def per_device(
@@ -366,7 +356,7 @@
             pltpu.VMEM((parts, n, part_size, entries), BF),
             pltpu.VMEM((parts * part_size, wall, entries), BF),
             pltpu.VMEM((wall, nchol), F32),
-            pltpu.VMEM((halves, nch, wall, chunk), F32),
+            pltpu.VMEM((halves, n, wrows, chunk), F32),
             pltpu.VMEM((halves, n, wrows, chunk), F32),
             pltpu.VMEM((halves, wrows, chunk), F32),
             pltpu.VMEM((halves, n, wrows, chunk), F32),
@@ -382,11 +372,11 @@
             pltpu.VMEM(walkers.shape[1:], BF),
             pltpu.VMEM(walkers.shape[1:], F32),
             dma((parts, halves)),
-            dma((parts, n)), dma((parts, n)),
-            dma((halves, n)), dma((halves, n)),
-            dma((halves, n)), dma((halves, n)),
-            dma((nch,)), dma((nch,)),
-            dma((parts, n)), dma((parts, n)),
+            dma((parts,)), dma((parts,)),
+            dma((halves,)), dma((halves,)),
+            dma((halves,)), dma((halves,)),
+            dma, dma,
+            dma((parts,)), dma((parts,)),
         ],
         compiler_params=pltpu.CompilerParams(
             collective_id=0, has_side_effects=True, vmem_limit_bytes=56 * 2**20

time: 53.6 us -> 51 us (0.951)
  Pallas kernels: 49.3 us -> 46.8 us
    pallas_call x1, Pallas kernels: 49.3 us -> 46.8 us  [per_device(): pl.pallas_call(functools.partial(kernel, n, cap, part_size, halves, chunk...]
where the time goes in v3:
time: 51 us; the launch traced here: 50.9 us
  Pallas kernels  46.8 us (92%)
  between operations  2.41 us (5%)
  local copies, waits for them, and re-layouts  1.67 us (3%)
    pallas_call x1, Pallas kernels, per_device(): pl.pallas_call(functools.partial(kernel, n, cap, part_size, halves, chunk...  46.8 us
    unnamed x1, local copies, waits for them, and re-layouts  1.67 us

profile of v3, /device:TPU:0, one launch (start us, length us, event | category | flops | bytes accessed | tf_op | source)
XLA Modules:
  0.0 50.9 jit_solution(15682246855998248849)
XLA Ops:
  0.6 46.8 %shard_map.104 = (bf16[1,512,256]{2,1,0:T(8,128)(2,1)}, f32[1]{0:T(128)}) custom-call(bf16[1,512,256]{2,1,0:T(8,128)(2,1)} %walk_ref.1, bf16[1,512,256]{2,1,0:T(8,128)(2,1)} %factor_ref.1, bf16[512,256]{1,0:T(8,128)(2,1)} %trial_ref.1, bf16[31,2048,256]{2,1,0:T(8,128)(2,1)} %chol_ref.1, s32[1,256]{1,0:T(1,128)} %bitcast.3, s32[16]{0:T(128)} %counts_ref.1, ...), custom_call_target="tpu_custom_call" | custom-call | flops 1040187392 | bytes 32505856 | tf_op jit(solution)/shard_map/pallas_call | solution.py:343
  47.4 1.7 %copy.13 = bf16[1,512,256]{2,1,0:T(8,128)(2,1)} copy(bf16[1,512,256]{2,1,0:T(8,128)(2,1)} %get-tuple-element.4) | data formatting | bytes 524288

commit v4 on v3

--- a/solution.py
+++ b/solution.py
@@ -46,12 +46,12 @@
 
 def kernel(
     n, cap, part_size, halves, chunk,
-    walk_ref, factor_ref, trial_ref, chol_ref, pattern_ref, counts_ref, cgroup_ref, gweight_ref,
-    aux_ref,
+    walk_hbm, factor_hbm, trial_hbm, chol_ref, pattern_ref, counts_ref, cgroup_ref, gweight_ref,
+    aux_hbm,
     adv_ref, lw_ref,
-    chol_v, spots, green_v, sent, got, tiles_v, bias_acc, part, part_got, field_own, field_got,
+    walk_ref, factor_ref, trial_ref, aux_ref, chol_v, spots, green_v, sent, got, tiles_v, bias_acc, part, part_got, field_own, field_got,
     field_all, fields_v, logw_own, logw_got, pot_acc, pot_v, back, back_got, v_mat, term_v, running_v,
-    chol_sem, a_send, a_recv, r_send, r_recv, f_send, f_recv, l_send, l_recv, b_send, b_recv,
+    in_sem, chol_sem, a_send, a_recv, r_send, r_recv, f_send, f_recv, l_send, l_recv, b_send, b_recv,
 ):
     me = lax.axis_index("tile")
     orbitals = walk_ref.shape[1]
@@ -86,6 +86,19 @@
         pl.semaphore_signal(
             barrier, inc=1, device_id={"tile": dst}, device_id_type=pl.DeviceIdType.MESH
         )
+    in_copies = [
+        pltpu.make_async_copy(src, dst, in_sem.at[i])
+        for i, (src, dst) in enumerate(
+            (
+                (factor_hbm, factor_ref),
+                (trial_hbm, trial_ref),
+                (walk_hbm, walk_ref),
+                (aux_hbm, aux_ref),
+            )
+        )
+    ]
+    for copy in in_copies:
+        copy.start()
     span = [(jp * part_size, min(cap, (jp + 1) * part_size)) for jp in range(parts)]
     chol_copies = {}
     for jp, (j0, j1) in enumerate(span):
@@ -98,7 +111,9 @@
                 chol_copies[jp, h].start()
 
     perm = swap_matrix(side, NBLK)
+    in_copies[0].wait()
     factor = dot(perm, factor_ref[0]).astype(BF)
+    in_copies[1].wait()
     green = lax.dot_general(
         factor, trial_ref[...], NT_DIMS, preferred_element_type=F32
     ).astype(BF)
@@ -153,6 +168,8 @@
                 chol_copies[jp + 1, h].start()
         got[jp, me] = sent[jp, me]
 
+    for copy in in_copies[2:]:
+        copy.wait()
     logw_parts = []
 
     def over_tiles(j0, j1, body, carry):
@@ -304,7 +321,9 @@
     running_v[...] = walk_ref[0].astype(F32)
 
     def taylor(degree, carry):
-        term = (dot(v_mat[...], term_v[...]) / degree.astype(F32)).astype(BF)
+        inverse = jnp.where(degree == 3, jnp.float32(1.0 / 3.0), jnp.float32(0.25))
+        inverse = jnp.where(degree == 1, 1.0, jnp.where(degree == 2, 0.5, inverse))
+        term = (dot(v_mat[...], term_v[...]) * inverse).astype(BF)
         term_v[...] = term
         running_v[...] = running_v[...] + term.astype(F32)
         return carry
@@ -340,15 +359,20 @@
     dma = pltpu.SemaphoreType.DMA
     vmem = pl.BlockSpec(memory_space=pltpu.VMEM)
     smem = pl.BlockSpec(memory_space=pltpu.SMEM)
+    far = pl.BlockSpec(memory_space=pl.ANY)
     advanced, log_weight = pl.pallas_call(
         functools.partial(kernel, n, cap, part_size, halves, chunk),
         out_shape=(
             jax.ShapeDtypeStruct(walkers.shape, BF),
             jax.ShapeDtypeStruct((1,), F32),
         ),
-        in_specs=[vmem, vmem, vmem, pl.BlockSpec(memory_space=pl.ANY), vmem, smem, vmem, smem, vmem],
+        in_specs=[far, far, far, far, vmem, smem, vmem, smem, far],
         out_specs=(vmem, smem),
         scratch_shapes=[
+            pltpu.VMEM(walkers.shape, BF),
+            pltpu.VMEM(green_factor.shape, BF),
+            pltpu.VMEM(trial.shape, BF),
+            pltpu.VMEM(aux.shape, jnp.int32),
             pltpu.VMEM((cap, nchol, entries), BF),
             pltpu.VMEM((entries, side * chunk), BF),
             pltpu.VMEM((orbitals // chunk * NBLK, side * chunk), BF),
@@ -371,6 +395,7 @@
             pltpu.VMEM((orbitals, orbitals), BF),
             pltpu.VMEM(walkers.shape[1:], BF),
             pltpu.VMEM(walkers.shape[1:], F32),
+            dma((4,)),
             dma((parts, halves)),
             dma((parts,)), dma((parts,)),
             dma((halves,)), dma((halves,)),

time: 51 us -> 51.3 us (level)
  no operation moved by 1% of the time
where the time goes in v4:
time: 51.3 us; the launch traced here: 51.1 us
  Pallas kernels  47 us (92%)
  between operations  2.41 us (5%)
  local copies, waits for them, and re-layouts  1.67 us (3%)
    pallas_call x1, Pallas kernels, per_device(): pl.pallas_call(functools.partial(kernel, n, cap, part_size, halves, chunk...  47 us
    unnamed x1, local copies, waits for them, and re-layouts  1.67 us

profile of v4, /device:TPU:0, one launch (start us, length us, event | category | flops | bytes accessed | tf_op | source)
XLA Modules:
  0.0 51.1 jit_solution(14966299310621500130)
XLA Ops:
  0.6 47.0 %shard_map.104 = (bf16[1,512,256]{2,1,0:T(8,128)(2,1)}, f32[1]{0:T(128)}) custom-call(bf16[1,512,256]{2,1,0:T(8,128)(2,1)} %walk_hbm.1, bf16[1,512,256]{2,1,0:T(8,128)(2,1)} %factor_hbm.1, bf16[512,256]{1,0:T(8,128)(2,1)} %trial_hbm.1, bf16[31,2048,256]{2,1,0:T(8,128)(2,1)} %chol_ref.1, s32[1,256]{1,0:T(1,128)} %bitcast.3, s32[16]{0:T(128)} %counts_ref.1, ...), custom_call_target="tpu_custom_call" | custom-call | flops 1040187392 | bytes 32505856 | tf_op jit(solution)/shard_map/pallas_call | solution.py:363
  47.6 1.7 %copy.13 = bf16[1,512,256]{2,1,0:T(8,128)(2,1)} copy(bf16[1,512,256]{2,1,0:T(8,128)(2,1)} %get-tuple-element.4) | data formatting | bytes 524288

commit v5 on v3

--- a/solution.py
+++ b/solution.py
@@ -67,7 +67,8 @@
     parts = -(-cap // part_size)
     rows = n * part_size
     mine_k = lax.rem(me, nch)
-    others = [lax.rem(me + off, n) for off in range(1, n)]
+    offsets = sorted(range(1, n), key=lambda off: (abs(off - n // 2), off))
+    others = [lax.rem(me + off, n) for off in offsets]
 
     def send(src, dst, ssem, rsem, dev):
         return pltpu.make_async_remote_copy(

time: 51 us -> 52.7 us (1.033)
  Pallas kernels: 46.8 us -> 48.4 us
    pallas_call x1, Pallas kernels: 46.8 us -> 48.4 us  [per_device(): pl.pallas_call(functools.partial(kernel, n, cap, part_size, halves, chunk...]
where the time goes in v5:
time: 52.7 us; the launch traced here: 52.5 us
  Pallas kernels  48.4 us (92%)
  between operations  2.41 us (5%)
  local copies, waits for them, and re-layouts  1.67 us (3%)
    pallas_call x1, Pallas kernels, per_device(): pl.pallas_call(functools.partial(kernel, n, cap, part_size, halves, chunk...  48.4 us
    unnamed x1, local copies, waits for them, and re-layouts  1.67 us

profile of v5, /device:TPU:0, one launch (start us, length us, event | category | flops | bytes accessed | tf_op | source)
XLA Modules:
  0.0 52.5 jit_solution(1067113936168280756)
XLA Ops:
  0.6 48.4 %shard_map.104 = (bf16[1,512,256]{2,1,0:T(8,128)(2,1)}, f32[1]{0:T(128)}) custom-call(bf16[1,512,256]{2,1,0:T(8,128)(2,1)} %walk_ref.1, bf16[1,512,256]{2,1,0:T(8,128)(2,1)} %factor_ref.1, bf16[512,256]{1,0:T(8,128)(2,1)} %trial_ref.1, bf16[31,2048,256]{2,1,0:T(8,128)(2,1)} %chol_ref.1, s32[1,256]{1,0:T(1,128)} %bitcast.3, s32[16]{0:T(128)} %counts_ref.1, ...), custom_call_target="tpu_custom_call" | custom-call | flops 1040187392 | bytes 32505856 | tf_op jit(solution)/shard_map/pallas_call | solution.py:344
  49.0 1.7 %copy.13 = bf16[1,512,256]{2,1,0:T(8,128)(2,1)} copy(bf16[1,512,256]{2,1,0:T(8,128)(2,1)} %get-tuple-element.4) | data formatting | bytes 524288
